TPU v7x, 128 devices: a whole 4x4x4 slice. The times are simulated.
128 devices in a mesh: pair: 2 (over x_hi), day: 16 (over z, y), lag: 4 (over x_lo, core).
Axes of the slice: x: 4 (x_hi: 2, x_lo: 2; x = x_hi * 2 + x_lo), y: 4, z: 4, core: 2. Of those that a mesh axis runs over, the one named last changes fastest.
Arguments:
- corr: bfloat16 [2048, 64, 2048], P('pair', 'day', 'lag'), may hold values from -150 to 150
Outputs:
- pws_stack: float32 [2048, 2048], P('pair', 'lag')
- robust_stack: float32 [2048, 2048], P('pair', 'lag')
- day_weights: float32 [2048, 64], P('pair', 'day')
All inputs are finite; a program needn't handle non-finite values.
Results may differ from a plain program's by a relative error of at most 0.00049.
Values may be sent and summed in bfloat16 or wider, within the bound.
A program may use at most 128 MiB of HBM per device.

v0:
```python
import jax
import jax.numpy as jnp
from jax import lax
from jax.sharding import PartitionSpec as P

ITERS = 3
epsilon = 1e-06


def kernel_block(rows, cols, lags):
    offset = (cols[None, :] - rows[:, None]) % lags
    odd = offset % 2 == 1
    angle = jnp.pi * offset.astype(jnp.float32) / lags
    value = jnp.where(odd, 2.0 / lags * jnp.cos(angle) / jnp.where(odd, jnp.sin(angle), 1.0), 0.0)
    return value.astype(jnp.bfloat16)


def per_device(corr):
    width_in = corr.shape[2]
    lags = width_in * lax.axis_size("lag")
    pairs, days_here, width = corr.shape
    days = days_here * lax.axis_size("day")
    data = corr.astype(jnp.float32)
    squares = jnp.sum(data * data, axis=2)
    norm2 = lax.psum(squares, "lag")
    rms = jnp.sqrt(norm2 / lags + epsilon)
    xn = data / rms[:, :, None]
    local_lags = lax.axis_index("lag") * width + jnp.arange(width, dtype=jnp.int32)
    piece = lax.all_gather(corr, "lag", axis=2, tiled=True)
    count = piece.shape[2]
    rows = jnp.arange(count, dtype=jnp.int32)
    block = kernel_block(rows, local_lags, lags)
    quad = jnp.dot(
        piece.reshape(pairs * days_here, count), block, preferred_element_type=jnp.float32
    )
    quad = quad.reshape(pairs, days_here, width)
    den = jnp.maximum(jnp.sqrt(data * data + quad * quad), 0.1 * rms[:, :, None])
    cosine = data / den
    sine = quad / den
    linear, csum, ssum = lax.psum(
        (jnp.sum(xn, axis=1), jnp.sum(cosine, axis=1), jnp.sum(sine, axis=1)), "day"
    )
    pws = linear / days * ((csum * csum + ssum * ssum) / (days * days))
    stack = pws
    for step in range(ITERS):
        energy = jnp.sum(stack * stack, axis=1)
        msq = lax.psum(energy, "lag") / lags
        normed = stack / jnp.sqrt(msq + epsilon)[:, None]
        inner = jnp.sum(xn * normed[:, None, :], axis=2)
        coh = lax.psum(inner, "lag") / lags
        spread = jnp.sum((xn - coh[:, :, None] * normed[:, None, :]) ** 2, axis=2)
        res = lax.psum(spread, "lag") / lags
        rbar = lax.psum(jnp.sum(res, axis=1), "day") / days
        weight = (0.1 + jnp.abs(coh)) / (res + rbar[:, None] + epsilon)
        stack, total = lax.psum(
            (jnp.sum(weight[:, :, None] * xn, axis=1), jnp.sum(weight, axis=1)), "day"
        )
    robust = stack / total[:, None]
    shares = weight / total[:, None]
    return (pws, robust, shares)


def solution(mesh):
    return jax.shard_map(
        per_device,
        mesh=mesh,
        in_specs=(P("pair", "day", "lag"),),
        out_specs=(P("pair", "lag"), P("pair", "lag"), P("pair", "day")),
        check_vma=False,
    )
```

profile of v0, /device:TPU:0, one launch (start us, length us, event | category | flops | bytes accessed | tf_op | source)
XLA Modules:
  0.0 961.6 jit_solution(4867787955644400862)
XLA Ops:
  7.2 0.7 all-gather.2.cloned.1.call-update
  7.9 4.5 fusion.1
  12.4 17.1 %psum.140 = f32[1024,4]{1,0:T(8,128)S(1)} all-reduce(f32[1024,4]{1,0:T(8,128)S(1)} %fusion.1), channel_id=1, replica_groups=mesh['pair'=2,'day'=16,'lag'=4] {'lag'}, use_global_device_ids=true, to_apply=%region_1.0 | all-reduce | flops 4096 | bytes 32768 | tf_op jit(solution)/shard_map/psum | solution.py:25
  29.7 19.0 %select_convert_fusion.4 = bf16[2048,512]{1,0:T(8,128)(2,1)S(1)} fusion(s32[512]{0:T(512)S(1)} %iota_add_fusion), kind=kLoop, calls=%fused_computation.28.clone.clone.1 | loop fusion | flops 32505856 | bytes 2099200 | tf_op jit(solution)/shard_map/dot_general | solution.py:33
  48.8 113.7 %all-gather.2.cloned.1.call-done = bf16[1024,4,2048]{2,1,0:T(4,128)(2,1)} async-done(((bf16[1024,4,512]{2,1,0:T(4,128)(2,1)}), bf16[1024,4,2048]{2,1,0:T(4,128)(2,1)}) %all-gather.2.cloned.1.call-update) | async-done | bytes 16777232 | tf_op jit(solution)/shard_map/all_gather | solution.py:29
  162.5 23.7 %reshape.35 = bf16[4096,2048]{1,0:T(8,128)(2,1)} reshape(bf16[1024,4,2048]{2,1,0:T(4,128)(2,1)} %all-gather.2.cloned.1.call-done) | data formatting | bytes 33554432 | tf_op jit(solution)/shard_map/reshape | solution.py:34
  186.1 14.5 %convolution_bitcast_fusion = f32[4096,512]{0,1:T(8,128)} fusion(bf16[4096,2048]{1,0:T(8,128)(2,1)} %reshape.35, bf16[2048,512]{1,0:T(8,128)(2,1)S(1)} %select_convert_fusion.4), kind=kOutput, calls=%fused_computation.18 | convolution fusion | flops 8589934592 | bytes 27262976 | tf_op jit(solution)/shard_map/dot_general | solution.py:33
  200.7 9.0 copy.24
  209.7 9.8 %reshape.36 = f32[1024,4,512]{2,1,0:T(4,128)} reshape(f32[4096,512]{1,0:T(8,128)} %copy.24) | data formatting | bytes 16777216 | tf_op jit(solution)/shard_map/reshape | solution.py:36
  219.5 32.9 %fusion.34 = (f32[1024,512]{1,0:T(8,128)}, f32[1024,4,512]{2,1,0:T(4,128)}, f32[1024,512]{1,0:T(8,128)}, f32[1024,512]{1,0:T(8,128)}) fusion(f32[1024,4]{1,0:T(8,128)S(1)} %get-tuple-element.19, bf16[1024,4,512]{2,1,0:T(4,128)(2,1)} %param.1, f32[1024,4,512]{2,1,0:T(4,128)} %reshape.36, f32[1024,4]{1,0:T(8,128)S(1)} %get-tuple-element.20), kind=kLoop, calls=%fused_computation.82 | loop fusion | flops 21495808 | bytes 27295744 | tf_op jit(solution)/shard_map/reduce_sum | solution.py:41
  252.5 125.8 %all-reduce.12.cloned.1.call-done = (f32[1024,512]{1,0:T(8,128)}, f32[1024,512]{1,0:T(8,128)}, f32[1024,512]{1,0:T(8,128)}) async-done(((f32[1024,512]{1,0:T(8,128)}, f32[1024,512]{1,0:T(8,128)}, f32[1024,512]{1,0:T(8,128)}), (f32[1024,512]{1,0:T(8,128)}, f32[1024,512]{1,0:T(8,128)}, f32[1024,512]{1,0:T(8,128)})) %all-reduce.12.cloned.1.call-update) | async-done | bytes 6291472 | tf_op jit(solution)/shard_map/psum | solution.py:40
  378.3 4.7 multiply_reduce_fusion.11
  383.0 6.8 psum.144
  389.8 1.8 broadcast_divide_fusion.3
  391.6 5.7 multiply_reduce_fusion.8
  397.3 16.0 %psum.145 = f32[1024,4]{1,0:T(8,128)S(1)} all-reduce(f32[1024,4]{1,0:T(8,128)S(1)} %multiply_reduce_fusion.8), channel_id=1, replica_groups=mesh['pair'=2,'day'=16,'lag'=4] {'lag'}, use_global_device_ids=true, to_apply=%region_11.12 | all-reduce | flops 4096 | bytes 32768 | tf_op jit(solution)/shard_map/psum | solution.py:50
  413.4 7.1 multiply_reduce_fusion.7
  420.5 16.3 %psum.146 = f32[1024,4]{1,0:T(8,128)S(1)} all-reduce(f32[1024,4]{1,0:T(8,128)S(1)} %multiply_reduce_fusion.7), channel_id=1, replica_groups=mesh['pair'=2,'day'=16,'lag'=4] {'lag'}, use_global_device_ids=true, to_apply=%region_13.14 | all-reduce | flops 4096 | bytes 32768 | tf_op jit(solution)/shard_map/psum | solution.py:52
  437.0 38.4 %psum.147 = f32[1024]{0:T(1024)S(1)} all-reduce(f32[1024]{0:T(1024)S(1)} %multiply_reduce_fusion.14), channel_id=1, replica_groups=mesh['pair'=2,'day'=16,'lag'=4] {'day'}, use_global_device_ids=true, to_apply=%region_15.16 | all-reduce | flops 1024 | bytes 8192 | tf_op jit(solution)/shard_map/psum | solution.py:53
  475.5 0.2 add_divide_fusion.1
  475.7 9.3 multiply_reduce_fusion.6
  485.1 86.2 %all-reduce.6.cloned.1.call-done = f32[1024,512]{1,0:T(8,128)} async-done(((f32[1024,512]{1,0:T(8,128)}), f32[1024,512]{1,0:T(8,128)}) %all-reduce.6.cloned.1.call-update) | async-done | bytes 2097168 | tf_op jit(solution)/shard_map/psum | solution.py:55
  571.3 1.8 multiply_reduce_fusion.10
  573.1 5.8 psum.149
  579.0 1.8 broadcast_divide_fusion.2
  580.8 5.7 multiply_reduce_fusion.5
  586.4 16.7 %psum.150 = f32[1024,4]{1,0:T(8,128)S(1)} all-reduce(f32[1024,4]{1,0:T(8,128)S(1)} %multiply_reduce_fusion.5), channel_id=1, replica_groups=mesh['pair'=2,'day'=16,'lag'=4] {'lag'}, use_global_device_ids=true, to_apply=%region_21.22 | all-reduce | flops 4096 | bytes 32768 | tf_op jit(solution)/shard_map/psum | solution.py:50
  603.2 7.1 multiply_reduce_fusion.4
  610.4 16.4 %psum.151 = f32[1024,4]{1,0:T(8,128)S(1)} all-reduce(f32[1024,4]{1,0:T(8,128)S(1)} %multiply_reduce_fusion.4), channel_id=1, replica_groups=mesh['pair'=2,'day'=16,'lag'=4] {'lag'}, use_global_device_ids=true, to_apply=%region_23.24 | all-reduce | flops 4096 | bytes 32768 | tf_op jit(solution)/shard_map/psum | solution.py:52
  626.9 38.2 %psum.152 = f32[1024]{0:T(1024)S(1)} all-reduce(f32[1024]{0:T(1024)S(1)} %multiply_reduce_fusion.13), channel_id=1, replica_groups=mesh['pair'=2,'day'=16,'lag'=4] {'day'}, use_global_device_ids=true, to_apply=%region_25.26 | all-reduce | flops 1024 | bytes 8192 | tf_op jit(solution)/shard_map/psum | solution.py:53
  665.1 0.2 add_divide_fusion
  665.3 9.3 multiply_reduce_fusion.3
  674.7 86.7 %all-reduce.8.cloned.1.call-done = f32[1024,512]{1,0:T(8,128)} async-done(((f32[1024,512]{1,0:T(8,128)}), f32[1024,512]{1,0:T(8,128)}) %all-reduce.8.cloned.1.call-update) | async-done | bytes 2097168 | tf_op jit(solution)/shard_map/psum | solution.py:55
  761.4 1.8 multiply_reduce_fusion.9
  763.2 5.7 psum.154
  768.9 1.8 broadcast_divide_fusion.1
  770.7 5.7 multiply_reduce_fusion.2
  776.4 16.7 %psum.155 = f32[1024,4]{1,0:T(8,128)S(1)} all-reduce(f32[1024,4]{1,0:T(8,128)S(1)} %multiply_reduce_fusion.2), channel_id=1, replica_groups=mesh['pair'=2,'day'=16,'lag'=4] {'lag'}, use_global_device_ids=true, to_apply=%region_31.32 | all-reduce | flops 4096 | bytes 32768 | tf_op jit(solution)/shard_map/psum | solution.py:50
  793.2 7.1 multiply_reduce_fusion.1
  800.3 16.6 %psum.156 = f32[1024,4]{1,0:T(8,128)S(1)} all-reduce(f32[1024,4]{1,0:T(8,128)S(1)} %multiply_reduce_fusion.1), channel_id=1, replica_groups=mesh['pair'=2,'day'=16,'lag'=4] {'lag'}, use_global_device_ids=true, to_apply=%region_33.34 | all-reduce | flops 4096 | bytes 32768 | tf_op jit(solution)/shard_map/psum | solution.py:52
  817.1 38.2 %psum.157 = f32[1024]{0:T(1024)S(1)} all-reduce(f32[1024]{0:T(1024)S(1)} %multiply_reduce_fusion.12), channel_id=1, replica_groups=mesh['pair'=2,'day'=16,'lag'=4] {'day'}, use_global_device_ids=true, to_apply=%region_35.36 | all-reduce | flops 1024 | bytes 8192 | tf_op jit(solution)/shard_map/psum | solution.py:53
  855.3 0.4 fusion.32
  855.6 9.3 multiply_reduce_fusion
  865.0 35.7 %psum.159 = f32[1024]{0:T(1024)S(1)} all-reduce(f32[1024]{0:T(1024)S(1)} %get-tuple-element.11), channel_id=1, replica_groups=mesh['pair'=2,'day'=16,'lag'=4] {'day'}, use_global_device_ids=true, to_apply=%region_39.40 | all-reduce | flops 1024 | bytes 8192 | tf_op jit(solution)/shard_map/psum | solution.py:55
  900.6 0.3 multiply_divide_fusion
  901.0 0.8 copy.25
  901.8 50.0 %all-reduce.10.cloned.1.call-done = f32[1024,512]{1,0:T(8,128)} async-done(((f32[1024,512]{1,0:T(8,128)}), f32[1024,512]{1,0:T(8,128)}) %all-reduce.10.cloned.1.call-update) | async-done | bytes 2097168 | tf_op jit(solution)/shard_map/psum | solution.py:55
  951.8 3.1 broadcast_divide_fusion
  (23 shorter events, 1.2 us)
Async XLA Ops:
  7.2 155.3 %all-gather.2.cloned.1.call-start = ((), (), s32[]{:S(2)}) async-start(), calls=%async_computation | async-start | bytes 20971520 | tf_op jit(solution)/shard_map/all_gather | solution.py:29
  7.9 370.4 %all-reduce.12.cloned.1.call-start = ((), (), s32[]{:S(2)}) async-start(), calls=%async_computation.4 | async-start | bytes 12582912 | tf_op jit(solution)/shard_map/psum | solution.py:40
  252.4 318.9 %all-reduce.6.cloned.1.call-start = ((), (), s32[]{:S(2)}) async-start(), calls=%async_computation.1 | async-start | bytes 4194304 | tf_op jit(solution)/shard_map/psum | solution.py:55
  485.0 276.4 %all-reduce.8.cloned.1.call-start = ((), (), s32[]{:S(2)}) async-start(), calls=%async_computation.2 | async-start | bytes 4194304 | tf_op jit(solution)/shard_map/psum | solution.py:55
  674.7 277.1 %all-reduce.10.cloned.1.call-start = ((), (), s32[]{:S(2)}) async-start(), calls=%async_computation.3 | async-start | bytes 4194304 | tf_op jit(solution)/shard_map/psum | solution.py:55
Sparse Core Ops, SparseCore 0:
  9.6 152.7 all-gather.1
  252.6 125.6 all-reduce.11
  485.1 86.1 all-reduce.5
  674.8 86.5 all-reduce.7
  865.1 86.6 all-reduce.9
where the time goes:
time: 972 us; the launch traced here: 962 us
  waiting for transfers between devices  463 us (48%)
  blocking collectives  285 us (29%)
  other arithmetic  142 us (15%)
  local copies, waits for them, and re-layouts  43.3 us (4%)
  matrix products  14.5 us (1%)
  between operations  14.2 us (1%)
    psum x3, waiting for transfers between devices, per_device(): lax.psum((jnp.sum(weight[:, :, None] * xn, axis=1), jnp.sum(weight, axis=...  223 us
    psum x1, waiting for transfers between devices, per_device(): lax.psum((jnp.sum(xn, axis=1), jnp.sum(cosine, axis=1), jnp.sum(sine, axi...  126 us
    psum x3, blocking collectives, per_device(): rbar = lax.psum(jnp.sum(res, axis=1), 'day') / days  115 us
    all_gather x1, waiting for transfers between devices, per_device(): piece = lax.all_gather(corr, 'lag', axis=2, tiled=True)  114 us
    psum x3, blocking collectives, per_device(): coh = lax.psum(inner, 'lag') / lags  49.5 us
    psum x3, blocking collectives, per_device(): res = lax.psum(spread, 'lag') / lags  49.3 us
    psum x1, blocking collectives, per_device(): lax.psum((jnp.sum(weight[:, :, None] * xn, axis=1), jnp.sum(weight, axis=...  35.7 us
    reduce_sum x1, other arithmetic, per_device(): jnp.sum(xn, axis=1)  32.9 us
  transfers between devices with their start and end apart: 5, of which 5 were waited for; matrix products, arithmetic and copies ran while one was open for 3% of the time, Pallas kernels for 0%

commit v1 on v0

--- a/solution.py
+++ b/solution.py
@@ -26,7 +26,9 @@
     rms = jnp.sqrt(norm2 / lags + epsilon)
     xn = data / rms[:, :, None]
     local_lags = lax.axis_index("lag") * width + jnp.arange(width, dtype=jnp.int32)
-    piece = lax.all_gather(corr, "lag", axis=2, tiled=True)
+    piece = jnp.concatenate(
+        lax.all_to_all(jnp.stack([corr] * lax.axis_size("lag")), "lag", 0, 0), axis=2
+    )
     count = piece.shape[2]
     rows = jnp.arange(count, dtype=jnp.int32)
     block = kernel_block(rows, local_lags, lags)

time: 972 us -> 1060 us (1.091)
  blocking collectives: 285 us -> 457 us
  waiting for transfers between devices: 463 us -> 348 us
  local copies, waits for them, and re-layouts: 43.3 us -> 72.7 us
    psum x1, blocking collectives: 17.1 us -> 190 us  [per_device(): norm2 = lax.psum(squares, 'lag')]
    all_gather x1 -> x0, waiting for transfers between devices: 114 us -> none  [per_device(): piece = lax.all_gather(corr, 'lag', axis=2, tiled=True)]
    reshape x1, local copies, waits for them, and re-layouts: 23.7 us -> 36.1 us  [per_device(): jnp.concatenate(lax.all_to_all(jnp.stack([corr] * lax.axis_size('lag')),...]
  transfers between devices with their start and end apart: 5 -> 5, of which waited for: 5 -> 4; matrix products, arithmetic and copies ran while one was open for 3% -> 2% of each run, Pallas kernels for 0% -> 0%
where the time goes in v1:
time: 1060 us
  blocking collectives  457 us (43%)
  waiting for transfers between devices  348 us (33%)
  other arithmetic  141 us (13%)
  local copies, waits for them, and re-layouts  72.7 us (7%)
  matrix products  14.5 us (1%)
  between operations  14.3 us (1%)
    psum x3, waiting for transfers between devices, per_device(): lax.psum((jnp.sum(weight[:, :, None] * xn, axis=1), jnp.sum(weight, axis=...  223 us
    psum x1, blocking collectives, per_device(): norm2 = lax.psum(squares, 'lag')  190 us
    psum x1, waiting for transfers between devices, per_device(): lax.psum((jnp.sum(xn, axis=1), jnp.sum(cosine, axis=1), jnp.sum(sine, axi...  125 us
    psum x3, blocking collectives, per_device(): rbar = lax.psum(jnp.sum(res, axis=1), 'day') / days  115 us
    psum x3, blocking collectives, per_device(): coh = lax.psum(inner, 'lag') / lags  49.5 us
    psum x3, blocking collectives, per_device(): res = lax.psum(spread, 'lag') / lags  49.3 us
    reshape x1, local copies, waits for them, and re-layouts, per_device(): jnp.concatenate(lax.all_to_all(jnp.stack([corr] * lax.axis_size('lag')),...  36.1 us
    psum x1, blocking collectives, per_device(): lax.psum((jnp.sum(weight[:, :, None] * xn, axis=1), jnp.sum(weight, axis=...  35.7 us
  transfers between devices with their start and end apart: 5, of which 4 were waited for; matrix products, arithmetic and copies ran while one was open for 2% of the time, Pallas kernels for 0%

profile of v1, /device:TPU:0, one launch (start us, length us, event | category | flops | bytes accessed | tf_op | source)
XLA Modules:
  0.0 1055.5 jit_solution(11511035023548413682)
XLA Ops:
  7.2 7.4 stack.2
  14.6 7.0 all-to-all-start
  21.6 4.5 fusion.1
  26.0 189.7 %psum.140 = f32[1024,4]{1,0:T(8,128)S(1)} all-reduce(f32[1024,4]{1,0:T(8,128)S(1)} %fusion.1), channel_id=1, replica_groups=mesh['pair'=2,'day'=16,'lag'=4] {'lag'}, use_global_device_ids=true, to_apply=%region_1.0 | all-reduce | flops 4096 | bytes 32768 | tf_op jit(solution)/shard_map/psum | solution.py:25
  215.9 19.0 %select_convert_fusion.4 = bf16[2048,512]{1,0:T(8,128)(2,1)S(1)} fusion(s32[512]{0:T(512)S(1)} %iota_add_fusion), kind=kLoop, calls=%fused_computation.28.clone.clone.1 | loop fusion | flops 32505856 | bytes 2099200 | tf_op jit(solution)/shard_map/dot_general | solution.py:35
  235.0 36.1 %copy.24 = bf16[1024,4,4,512]{3,2,1,0:T(4,128)(2,1)S(1)} copy(bf16[1024,4,4,512]{3,1,0,2:T(4,128)(2,1)} %bitcast) | data formatting | bytes 33554432 | tf_op jit(solution)/shard_map/reshape | solution.py:29
  271.1 9.4 copy.27
  280.5 14.5 %convolution_bitcast_fusion = f32[4096,512]{0,1:T(8,128)} fusion(bf16[4096,2048]{1,0:T(8,128)(2,1)} %bitcast.11, bf16[2048,512]{1,0:T(8,128)(2,1)S(1)} %select_convert_fusion.4), kind=kOutput, calls=%fused_computation.18 | convolution fusion | flops 8589934592 | bytes 27262976 | tf_op jit(solution)/shard_map/dot_general | solution.py:35
  295.1 9.0 copy.25
  304.1 10.0 reshape.38
  314.0 32.5 %fusion.34 = (f32[1024,512]{1,0:T(8,128)}, f32[1024,4,512]{2,1,0:T(4,128)}, f32[1024,512]{1,0:T(8,128)}, f32[1024,512]{1,0:T(8,128)}) fusion(f32[1024,4]{1,0:T(8,128)S(1)} %get-tuple-element.19, bf16[1024,4,512]{2,1,0:T(4,128)(2,1)} %param.1, f32[1024,4,512]{2,1,0:T(4,128)} %reshape.38, f32[1024,4]{1,0:T(8,128)S(1)} %get-tuple-element.20), kind=kLoop, calls=%fused_computation.82 | loop fusion | flops 21495808 | bytes 27295744 | tf_op jit(solution)/shard_map/reduce_sum | solution.py:43
  346.6 125.4 %all-reduce.12.cloned.1.call-done = (f32[1024,512]{1,0:T(8,128)}, f32[1024,512]{1,0:T(8,128)}, f32[1024,512]{1,0:T(8,128)}) async-done(((f32[1024,512]{1,0:T(8,128)}, f32[1024,512]{1,0:T(8,128)}, f32[1024,512]{1,0:T(8,128)}), (f32[1024,512]{1,0:T(8,128)}, f32[1024,512]{1,0:T(8,128)}, f32[1024,512]{1,0:T(8,128)})) %all-reduce.12.cloned.1.call-update) | async-done | bytes 6291472 | tf_op jit(solution)/shard_map/psum | solution.py:42
  472.0 4.7 multiply_reduce_fusion.11
  476.7 6.8 psum.144
  483.6 1.8 broadcast_divide_fusion.3
  485.4 5.7 multiply_reduce_fusion.8
  491.0 16.0 %psum.145 = f32[1024,4]{1,0:T(8,128)S(1)} all-reduce(f32[1024,4]{1,0:T(8,128)S(1)} %multiply_reduce_fusion.8), channel_id=1, replica_groups=mesh['pair'=2,'day'=16,'lag'=4] {'lag'}, use_global_device_ids=true, to_apply=%region_11.12 | all-reduce | flops 4096 | bytes 32768 | tf_op jit(solution)/shard_map/psum | solution.py:52
  507.1 7.1 multiply_reduce_fusion.7
  514.2 16.3 %psum.146 = f32[1024,4]{1,0:T(8,128)S(1)} all-reduce(f32[1024,4]{1,0:T(8,128)S(1)} %multiply_reduce_fusion.7), channel_id=1, replica_groups=mesh['pair'=2,'day'=16,'lag'=4] {'lag'}, use_global_device_ids=true, to_apply=%region_13.14 | all-reduce | flops 4096 | bytes 32768 | tf_op jit(solution)/shard_map/psum | solution.py:54
  530.8 38.4 %psum.147 = f32[1024]{0:T(1024)S(1)} all-reduce(f32[1024]{0:T(1024)S(1)} %multiply_reduce_fusion.14), channel_id=1, replica_groups=mesh['pair'=2,'day'=16,'lag'=4] {'day'}, use_global_device_ids=true, to_apply=%region_15.16 | all-reduce | flops 1024 | bytes 8192 | tf_op jit(solution)/shard_map/psum | solution.py:55
  569.4 9.3 multiply_reduce_fusion.6
  578.8 86.2 %all-reduce.6.cloned.1.call-done = f32[1024,512]{1,0:T(8,128)} async-done(((f32[1024,512]{1,0:T(8,128)}), f32[1024,512]{1,0:T(8,128)}) %all-reduce.6.cloned.1.call-update) | async-done | bytes 2097168 | tf_op jit(solution)/shard_map/psum | solution.py:57
  665.0 1.8 multiply_reduce_fusion.10
  666.9 5.9 psum.149
  672.7 1.8 broadcast_divide_fusion.2
  674.5 5.7 multiply_reduce_fusion.5
  680.2 16.7 %psum.150 = f32[1024,4]{1,0:T(8,128)S(1)} all-reduce(f32[1024,4]{1,0:T(8,128)S(1)} %multiply_reduce_fusion.5), channel_id=1, replica_groups=mesh['pair'=2,'day'=16,'lag'=4] {'lag'}, use_global_device_ids=true, to_apply=%region_21.22 | all-reduce | flops 4096 | bytes 32768 | tf_op jit(solution)/shard_map/psum | solution.py:52
  697.0 7.1 multiply_reduce_fusion.4
  704.1 16.4 %psum.151 = f32[1024,4]{1,0:T(8,128)S(1)} all-reduce(f32[1024,4]{1,0:T(8,128)S(1)} %multiply_reduce_fusion.4), channel_id=1, replica_groups=mesh['pair'=2,'day'=16,'lag'=4] {'lag'}, use_global_device_ids=true, to_apply=%region_23.24 | all-reduce | flops 4096 | bytes 32768 | tf_op jit(solution)/shard_map/psum | solution.py:54
  720.7 38.2 %psum.152 = f32[1024]{0:T(1024)S(1)} all-reduce(f32[1024]{0:T(1024)S(1)} %multiply_reduce_fusion.13), channel_id=1, replica_groups=mesh['pair'=2,'day'=16,'lag'=4] {'day'}, use_global_device_ids=true, to_apply=%region_25.26 | all-reduce | flops 1024 | bytes 8192 | tf_op jit(solution)/shard_map/psum | solution.py:55
  758.9 0.2 add_divide_fusion
  759.1 9.3 multiply_reduce_fusion.3
  768.5 86.7 %all-reduce.8.cloned.1.call-done = f32[1024,512]{1,0:T(8,128)} async-done(((f32[1024,512]{1,0:T(8,128)}), f32[1024,512]{1,0:T(8,128)}) %all-reduce.8.cloned.1.call-update) | async-done | bytes 2097168 | tf_op jit(solution)/shard_map/psum | solution.py:57
  855.2 1.8 multiply_reduce_fusion.9
  857.0 5.7 psum.154
  862.7 1.8 broadcast_divide_fusion.1
  864.5 5.7 multiply_reduce_fusion.2
  870.1 16.7 %psum.155 = f32[1024,4]{1,0:T(8,128)S(1)} all-reduce(f32[1024,4]{1,0:T(8,128)S(1)} %multiply_reduce_fusion.2), channel_id=1, replica_groups=mesh['pair'=2,'day'=16,'lag'=4] {'lag'}, use_global_device_ids=true, to_apply=%region_31.32 | all-reduce | flops 4096 | bytes 32768 | tf_op jit(solution)/shard_map/psum | solution.py:52
  886.9 7.1 multiply_reduce_fusion.1
  894.1 16.6 %psum.156 = f32[1024,4]{1,0:T(8,128)S(1)} all-reduce(f32[1024,4]{1,0:T(8,128)S(1)} %multiply_reduce_fusion.1), channel_id=1, replica_groups=mesh['pair'=2,'day'=16,'lag'=4] {'lag'}, use_global_device_ids=true, to_apply=%region_33.34 | all-reduce | flops 4096 | bytes 32768 | tf_op jit(solution)/shard_map/psum | solution.py:54
  910.9 38.2 %psum.157 = f32[1024]{0:T(1024)S(1)} all-reduce(f32[1024]{0:T(1024)S(1)} %multiply_reduce_fusion.12), channel_id=1, replica_groups=mesh['pair'=2,'day'=16,'lag'=4] {'day'}, use_global_device_ids=true, to_apply=%region_35.36 | all-reduce | flops 1024 | bytes 8192 | tf_op jit(solution)/shard_map/psum | solution.py:55
  949.1 0.4 fusion.32
  949.5 9.3 multiply_reduce_fusion
  958.8 35.7 %psum.159 = f32[1024]{0:T(1024)S(1)} all-reduce(f32[1024]{0:T(1024)S(1)} %get-tuple-element.11), channel_id=1, replica_groups=mesh['pair'=2,'day'=16,'lag'=4] {'day'}, use_global_device_ids=true, to_apply=%region_39.40 | all-reduce | flops 1024 | bytes 8192 | tf_op jit(solution)/shard_map/psum | solution.py:57
  994.5 0.3 multiply_divide_fusion
  994.8 0.8 copy.26
  995.6 50.0 %all-reduce.10.cloned.1.call-done = f32[1024,512]{1,0:T(8,128)} async-done(((f32[1024,512]{1,0:T(8,128)}), f32[1024,512]{1,0:T(8,128)}) %all-reduce.10.cloned.1.call-update) | async-done | bytes 2097168 | tf_op jit(solution)/shard_map/psum | solution.py:57
  1045.6 3.1 broadcast_divide_fusion
  (24 shorter events, 1.4 us)
Async XLA Ops:
  14.6 220.4 %all-to-all-start = ((bf16[4,1024,4,512]{3,2,1,0:T(4,128)(2,1)}), bf16[4,1024,4,512]{3,2,1,0:T(4,128)(2,1)}, u32[]{:S(2)}, u32[]{:S(2)}) async-start(bf16[4,1024,4,512]{3,2,1,0:T(4,128)(2,1)} %stack.2), calls=%async_computation | async-start | bytes 33554432 | tf_op jit(solution)/shard_map/all_to_all | solution.py:30
  21.5 450.5 %all-reduce.12.cloned.1.call-start = ((), (), s32[]{:S(2)}) async-start(), calls=%async_computation.4 | async-start | bytes 12582912 | tf_op jit(solution)/shard_map/psum | solution.py:42
  346.5 318.5 %all-reduce.6.cloned.1.call-start = ((), (), s32[]{:S(2)}) async-start(), calls=%async_computation.1 | async-start | bytes 4194304 | tf_op jit(solution)/shard_map/psum | solution.py:57
  578.8 276.4 %all-reduce.8.cloned.1.call-start = ((), (), s32[]{:S(2)}) async-start(), calls=%async_computation.2 | async-start | bytes 4194304 | tf_op jit(solution)/shard_map/psum | solution.py:57
  768.4 277.1 %all-reduce.10.cloned.1.call-start = ((), (), s32[]{:S(2)}) async-start(), calls=%async_computation.3 | async-start | bytes 4194304 | tf_op jit(solution)/shard_map/psum | solution.py:57
Sparse Core Ops, SparseCore 0:
  346.7 125.2 all-reduce.11
  578.9 86.1 all-reduce.5
  768.6 86.5 all-reduce.7
  958.9 86.6 all-reduce.9
